TPU v7x, 32 devices: a whole 2x2x4 slice. The times are simulated.
32 devices in a mesh: groups: 2 (over x), slab: 2 (over core), tm: 8 (over z, y).
Axes of the slice: x: 2, y: 2, z: 4, core: 2. Of those that a mesh axis runs over, the one named last changes fastest.
Arguments:
- demand: int32 [8, 256], P('groups', ('slab', 'tm')), parts along dimension 0, may hold values from 0 to 20
- lead_offset: int32 [8, 256], P('groups', ('slab', 'tm')), parts along dimension 0, may hold values from 0 to 7
- review: int32 [8, 256], P('groups', ('slab', 'tm')), parts along dimension 0, may hold values 0 or 1
- scenario_id: int32 [8], P('groups'), parts along dimension 0, may hold values from 0 to 15
- initial_state: float32 [8, 128], P('groups'), parts along dimension 0, may hold values from -2.5 to 2.5
- guess: float32 [8, 256, 128], P('groups', ('slab', 'tm')), parts along dimension 0, may hold values from -0.9 to 0.9
- input_weight: float32 [16, 384], replicated, may hold values from -1.5 to 1.5
- scenario_table: float32 [16, 384], replicated, may hold values from -3 to 3
- recur_weight: float32 [128, 384], replicated, may hold values from -0.5 to 0.5
- update_bias: float32 [128], replicated, may hold values from -1.5 to 10
- review_depth: float32 [128], replicated, may hold values from 0.8 to 0.95
Outputs:
- trajectory: float32 [8, 256, 128], P('groups', ('slab', 'tm')), parts along dimension 0
There are 2 independent parts, one for each index of `groups`. A program takes and returns all parts, laid end to end along the dimension named above; an argument that names none is the same for every part. Nothing has to cross between parts.
All inputs are finite; a program needn't handle non-finite values. No bound on the sum of `review` on one device may be relied on, other than what follows from the above.
Results may differ from a plain program's by a relative error of at most 0.0003.
Values sent between devices are 32-bit elements; how exact they have to be, the bound alone decides.
A program may use at most 128 MiB of HBM per device.

v0:
```python
import functools

import jax
import jax.numpy as jnp
from jax import lax
from jax.experimental import pallas as pl
from jax.experimental.pallas import tpu as pltpu
from jax.sharding import PartitionSpec as P

LEAD = 8
NEWTON = 2
EXACT = (True, True)
MESH = pl.DeviceIdType.MESH
F32 = jnp.float32
BF16 = jnp.bfloat16


def split(value):
    high = value.astype(BF16)
    return high, (value - high.astype(F32)).astype(BF16)


def dot(a, b):
    return jnp.dot(a, b, preferred_element_type=F32)


def dot3(value, w_high, w_low):
    high, low = split(value)
    return dot(high, w_high) + dot(low, w_high) + dot(high, w_low)


def through(column, matrix):
    return jnp.sum(column * matrix, axis=0, keepdims=True)


def column_of(row):
    hidden = row.shape[1]
    return jnp.transpose(jnp.broadcast_to(row, (hidden, hidden)))


def kernel(
    sid_ref, demand_ref, lead_ref, review_ref, init_ref, guess_ref, iw_ref, table_ref, rw_ref, ub_ref, depth_ref,
    out_ref,
    sbuf, held, old, wh, wl, xin, mult, co_z, co_cz, co_n, co_r, err, pre, aff, dsend, dtake, traj,
    send_sem, rim_sem, recv_sem, rim_recv, chain_send, chain_recv, out_send, out_recv,
):
    scen, periods, hidden = guess_ref.shape
    inner = lax.axis_size("tm")
    links = lax.axis_size("slab") * inner // scen
    place = lax.axis_index("slab") * inner + lax.axis_index("tm")
    link = place // scen
    mine = lax.rem(place, scen)
    rows = scen * periods

    def device(at_link, member):
        index = at_link * scen + member
        return {"slab": index // inner, "tm": lax.rem(index, inner)}

    def peer(step):
        return lax.rem(mine + step, scen)

    first = link == 0
    final = link == links - 1
    tail = mine == scen - 1

    barrier = pltpu.get_barrier_semaphore()
    for step in range(1, scen):
        pl.semaphore_signal(barrier, inc=1, device_id=device(link, peer(step)), device_id_type=MESH)

    @pl.when(jnp.logical_not(first))
    def _():
        pl.semaphore_signal(barrier, inc=1, device_id=device(link - 1, mine), device_id_type=MESH)

    @pl.when(jnp.logical_not(first) & jnp.logical_not(tail))
    def _():
        pl.semaphore_signal(barrier, inc=1, device_id=device(link - 1, scen - 1), device_id_type=MESH)

    square = (periods, periods)
    diagonal = lax.broadcasted_iota(jnp.int32, square, 0) == lax.broadcasted_iota(jnp.int32, square, 1)
    lane = lax.broadcasted_iota(jnp.int32, (periods, hidden), 1)

    def upright(row):
        picked = jnp.where(diagonal, jnp.broadcast_to(row, square), 0.0)
        return jnp.broadcast_to(jnp.sum(picked, axis=1, keepdims=True), (periods, hidden))

    for s in range(scen):
        demand = upright(demand_ref[s : s + 1, :].astype(F32))
        lead = upright(lead_ref[s : s + 1, :].astype(F32))
        review = upright(review_ref[s : s + 1, :].astype(F32))
        sbuf[s, :, :hidden] = guess_ref[s]
        sbuf[s, :, hidden:] = jnp.where(lane < LEAD, demand, jnp.where(lane < 2 * LEAD, lead, review))

    pl.semaphore_wait(
        barrier,
        (scen - 1) + jnp.where(final, 0, 1) + jnp.where(jnp.logical_not(final) & tail, scen - 1, 0),
    )

    def exchange(step):
        to = peer(step)
        return pltpu.make_async_remote_copy(
            src_ref=sbuf.at[to],
            dst_ref=held.at[pl.ds(pl.multiple_of(8 + mine * periods, 8), periods)],
            send_sem=send_sem.at[step],
            recv_sem=recv_sem.at[scen - step],
            device_id=device(link, to),
            device_id_type=MESH,
        )

    def arrival(step):
        source = peer(step)
        return pltpu.make_async_remote_copy(
            src_ref=sbuf.at[0],
            dst_ref=held.at[pl.ds(pl.multiple_of(8 + source * periods, 8), periods)],
            send_sem=send_sem.at[step],
            recv_sem=recv_sem.at[step],
            device_id=device(link, source),
            device_id_type=MESH,
        )

    def rim(member):
        return pltpu.make_async_remote_copy(
            src_ref=sbuf.at[member, pl.ds(periods - 8, 8)],
            dst_ref=held.at[pl.ds(0, 8)],
            send_sem=rim_sem.at[member],
            recv_sem=rim_recv,
            device_id=device(link + 1, member),
            device_id_type=MESH,
        )

    for step in range(1, scen):
        exchange(step).start()

    @pl.when(tail & jnp.logical_not(final))
    def _():
        for member in range(scen):
            rim(member).start()

    held[pl.ds(pl.multiple_of(8 + mine * periods, 8), periods), :] = sbuf[mine]

    @pl.when(first)
    def _():
        held[0:8, :hidden] = jnp.broadcast_to(init_ref[pl.ds(mine, 1), :], (8, hidden))
        held[0:8, hidden:] = jnp.zeros((8, hidden), F32)

    weights = rw_ref[...]
    w_high, w_low = split(weights)
    wh[...] = w_high
    wl[...] = w_low
    iw_high, iw_rest = split(iw_ref[...])
    iw_low = iw_rest
    table_row = table_ref[pl.ds(sid_ref[mine], 1), :]

    for step in range(1, scen):
        arrival(step).wait_recv()

    @pl.when(jnp.logical_not(first))
    def _():
        rim(0).wait_recv()

    lanes = lax.broadcasted_iota(jnp.int32, (rows, hidden), 1)
    feat = jnp.where(
        (lanes >= LEAD) & (lanes < 2 * LEAD) & (held[8:, hidden:] == (lanes - LEAD).astype(F32)), 1.0, 0.0
    )
    for j in range(LEAD):
        feat = jnp.where(lanes == j, held[8 - j : 8 - j + rows, hidden:] * 0.125, feat)
    feat = feat[:, : 2 * LEAD].astype(BF16)
    xin[...] = dot(feat, iw_high) + dot(feat, iw_low) + table_row
    review = jnp.broadcast_to(held[8:, 2 * hidden - 1 :], (rows, hidden))
    mult[...] = 1.0 - depth_ref[...] * review
    old[...] = held[:, :hidden]

    eye = jnp.where(
        lax.broadcasted_iota(jnp.int32, (hidden, hidden), 0) == lax.broadcasted_iota(jnp.int32, (hidden, hidden), 1),
        1.0,
        0.0,
    )
    pad = 16

    for turn in range(NEWTON):
        prior = old[7 : 7 + rows, :]
        recur = dot3(prior, wh[...], wl[...])
        m = mult[...]
        z = jax.nn.sigmoid((xin[:, :hidden] + recur[:, :hidden] + ub_ref[...]) * m)
        r = jax.nn.sigmoid(xin[:, hidden : 2 * hidden] + recur[:, hidden : 2 * hidden])
        un = recur[:, 2 * hidden :]
        n = jnp.tanh(xin[:, 2 * hidden :] + r * un)
        stay = 1.0 - z
        cn = stay * (1.0 - n * n) * r
        co_z[...] = z
        co_cz[...] = (prior - n) * z * stay * m
        co_n[...] = cn
        co_r[...] = cn * un * (1.0 - r)
        err[...] = stay * n + z * prior - old[8:, :]

        for b in range(scen):
            at = slice(b * periods, b * periods + 1)
            pre[0, b * hidden : (b + 1) * hidden, :] = (
                co_z[at, :] * eye
                + co_cz[at, :] * rw_ref[:, :hidden]
                + co_n[at, :] * rw_ref[:, 2 * hidden :]
                + co_r[at, :] * rw_ref[:, hidden : 2 * hidden]
            )
            aff[0, b : b + 1, :] = err[at, :]
        aff[0, scen:, :] = jnp.zeros((pad - scen, hidden), F32)

        def compose(t, carry):
            x = jnp.concatenate([pre[t - 1], aff[t - 1]], axis=0)
            if EXACT[turn]:
                moved = dot3(x, wh[...], wl[...])
            else:
                moved = dot(x.astype(BF16), wh[...])
            for b in range(scen):
                at = pl.ds(b * periods + t, 1)
                own = slice(b * hidden, (b + 1) * hidden)
                pre[t, own, :] = (
                    co_z[at, :] * x[own]
                    + co_cz[at, :] * moved[own, :hidden]
                    + co_n[at, :] * moved[own, 2 * hidden :]
                    + co_r[at, :] * moved[own, hidden : 2 * hidden]
                )
                row = slice(scen * hidden + b, scen * hidden + b + 1)
                aff[t, b : b + 1, :] = (
                    co_z[at, :] * x[row]
                    + co_cz[at, :] * moved[row, :hidden]
                    + co_n[at, :] * moved[row, 2 * hidden :]
                    + co_r[at, :] * moved[row, hidden : 2 * hidden]
                    + err[at, :]
                )
            aff[t, scen:, :] = jnp.zeros((pad - scen, hidden), F32)
            return carry

        lax.fori_loop(1, periods, compose, 0)

        onward = pltpu.make_async_remote_copy(
            src_ref=dsend.at[turn],
            dst_ref=dtake.at[turn],
            send_sem=chain_send.at[turn],
            recv_sem=chain_recv.at[turn],
            device_id=device(link + 1, mine),
            device_id_type=MESH,
        )

        @pl.when(first)
        def _():
            dtake[turn] = jnp.zeros((8, hidden), F32)

        @pl.when(jnp.logical_not(first))
        def _():
            onward.wait_recv()

        enter = dtake[turn, 0:1, :]
        entering = enter
        columns = []
        for b in range(scen):
            column = column_of(entering)
            columns.append(column)
            entering = aff[periods - 1, b : b + 1, :] + through(
                column, pre[periods - 1, b * hidden : (b + 1) * hidden, :]
            )
        dsend[turn] = jnp.broadcast_to(entering, (8, hidden))

        @pl.when(jnp.logical_not(final))
        def _():
            onward.start()

        target = old if turn + 1 < NEWTON else traj
        shift = 8 if turn + 1 < NEWTON else 0
        if turn + 1 < NEWTON:
            old[0:8, :] = old[0:8, :] + jnp.broadcast_to(enter, (8, hidden))
        for b in range(scen):
            for t in range(periods):
                at = b * periods + t
                target[shift + at : shift + at + 1, :] = (
                    old[8 + at : 9 + at, :]
                    + aff[t, b : b + 1, :]
                    + through(columns[b], pre[t, b * hidden : (b + 1) * hidden, :])
                )

    def back(step):
        to = peer(step)
        return pltpu.make_async_remote_copy(
            src_ref=traj.at[pl.ds(pl.multiple_of(to * periods, 8), periods)],
            dst_ref=out_ref.at[mine],
            send_sem=out_send.at[step],
            recv_sem=out_recv.at[scen - step],
            device_id=device(link, to),
            device_id_type=MESH,
        )

    def returned(step):
        source = peer(step)
        return pltpu.make_async_remote_copy(
            src_ref=traj.at[pl.ds(0, periods)],
            dst_ref=out_ref.at[source],
            send_sem=out_send.at[step],
            recv_sem=out_recv.at[step],
            device_id=device(link, source),
            device_id_type=MESH,
        )

    for step in range(1, scen):
        back(step).start()
    out_ref[mine] = traj[pl.ds(pl.multiple_of(mine * periods, 8), periods), :]

    for step in range(1, scen):
        exchange(step).wait_send()

    @pl.when(tail & jnp.logical_not(final))
    def _():
        for member in range(scen):
            rim(member).wait_send()

    @pl.when(jnp.logical_not(final))
    def _():
        for turn in range(NEWTON):
            pltpu.make_async_remote_copy(
                src_ref=dsend.at[turn],
                dst_ref=dtake.at[turn],
                send_sem=chain_send.at[turn],
                recv_sem=chain_recv.at[turn],
                device_id=device(link + 1, mine),
                device_id_type=MESH,
            ).wait_send()

    for step in range(1, scen):
        back(step).wait_send()
        returned(step).wait_recv()


def on_device(
    demand, lead_offset, review, scenario_id, initial_state, guess,
    input_weight, scenario_table, recur_weight, update_bias, review_depth,
):
    scen, periods, hidden = guess.shape
    rows = scen * periods
    vmem = pl.BlockSpec(memory_space=pltpu.VMEM)
    dma = pltpu.SemaphoreType.DMA
    tile = pltpu.VMEM((rows, hidden), F32)
    return pl.pallas_call(
        kernel,
        out_shape=jax.ShapeDtypeStruct(guess.shape, F32),
        in_specs=[pl.BlockSpec(memory_space=pltpu.SMEM)] + [vmem] * 10,
        out_specs=vmem,
        scratch_shapes=[
            pltpu.VMEM((scen, periods, 2 * hidden), F32),
            pltpu.VMEM((8 + rows, 2 * hidden), F32),
            pltpu.VMEM((8 + rows, hidden), F32),
            pltpu.VMEM((hidden, 3 * hidden), BF16),
            pltpu.VMEM((hidden, 3 * hidden), BF16),
            pltpu.VMEM((rows, 3 * hidden), F32),
            tile, tile, tile, tile, tile, tile,
            pltpu.VMEM((periods, scen * hidden, hidden), F32),
            pltpu.VMEM((periods, 16, hidden), F32),
            pltpu.VMEM((NEWTON, 8, hidden), F32),
            pltpu.VMEM((NEWTON, 8, hidden), F32),
            tile,
            dma((scen,)), dma((scen,)), dma((scen,)), dma(()), dma((NEWTON,)), dma((NEWTON,)), dma((scen,)), dma((scen,)),
        ],
        compiler_params=pltpu.CompilerParams(
            collective_id=0, has_side_effects=True, vmem_limit_bytes=40 * 1024 * 1024
        ),
        name="newton",
    )(
        scenario_id, demand, lead_offset, review, initial_state, guess, input_weight, scenario_table,
        recur_weight, update_bias[None], review_depth[None],
    )


def solution(mesh):
    return jax.shard_map(
        on_device,
        mesh=mesh,
        in_specs=(
            P("groups", ("slab", "tm")),
            P("groups", ("slab", "tm")),
            P("groups", ("slab", "tm")),
            P("groups"),
            P("groups", None),
            P("groups", ("slab", "tm"), None),
            P(),
            P(),
            P(),
            P(),
            P(),
        ),
        out_specs=P("groups", ("slab", "tm"), None),
        check_vma=False,
    )
```

profile of v0, /device:TPU:17, one launch (start us, length us, event | category | flops | bytes accessed | tf_op | source)
XLA Modules:
  0.0 43.8 jit_solution(3803149304238314477)
XLA Ops:
  0.0 0.0 copy-start.4
  0.0 0.0 copy-start.8
  0.0 0.0 copy-start.9
  0.0 0.0 copy-start.10
  0.0 0.7 %copy-done.4 = s32[4,16]{1,0:T(4,128)S(1)} copy-done((s32[4,16]{1,0:T(4,128)S(1)}, s32[4,16]{1,0:T(4,128)}, u32[]{:S(2)}) %copy-start.4) | copy-done | bytes 280
  0.7 0.0 copy-done.8
  0.7 0.0 copy-done.9
  0.7 0.0 copy-done.10
  0.7 0.0 copy-start
  0.7 0.9 %copy-done = f32[128,384]{1,0:T(8,128)S(1)} copy-done((f32[128,384]{1,0:T(8,128)S(1)}, f32[128,384]{1,0:T(8,128)}, u32[]{:S(2)}) %copy-start) | copy-done | bytes 196632
  1.6 0.0 copy-start.1
  1.6 0.8 %copy-done.1 = f32[4,16,128]{2,1,0:T(8,128)S(1)} copy-done((f32[4,16,128]{2,1,0:T(8,128)S(1)}, f32[4,16,128]{2,1,0:T(8,128)}, u32[]{:S(2)}) %copy-start.1) | copy-done | bytes 32792
  2.4 0.0 copy-start.2
  2.4 0.7 %copy-done.2 = f32[16,384]{1,0:T(8,128)S(1)} copy-done((f32[16,384]{1,0:T(8,128)S(1)}, f32[16,384]{1,0:T(8,128)}, u32[]{:S(2)}) %copy-start.2) | copy-done | bytes 24600
  3.1 0.0 copy-start.3
  3.1 0.7 %copy-done.3 = f32[16,384]{1,0:T(8,128)S(1)} copy-done((f32[16,384]{1,0:T(8,128)S(1)}, f32[16,384]{1,0:T(8,128)}, u32[]{:S(2)}) %copy-start.3) | copy-done | bytes 24600
  3.9 0.0 copy-start.5
  3.9 0.7 %copy-done.5 = s32[4,16]{1,0:T(4,128)S(1)} copy-done((s32[4,16]{1,0:T(4,128)S(1)}, s32[4,16]{1,0:T(4,128)}, u32[]{:S(2)}) %copy-start.5) | copy-done | bytes 280
  4.5 0.0 copy-start.6
  4.5 0.7 %copy-done.6 = s32[4,16]{1,0:T(4,128)S(1)} copy-done((s32[4,16]{1,0:T(4,128)S(1)}, s32[4,16]{1,0:T(4,128)}, u32[]{:S(2)}) %copy-start.6) | copy-done | bytes 280
  5.2 0.0 copy-start.7
  5.2 0.7 %copy-done.7 = f32[4,128]{1,0:T(4,128)S(1)} copy-done((f32[4,128]{1,0:T(4,128)S(1)}, f32[4,128]{1,0:T(4,128)}, u32[]{:S(2)}) %copy-start.7) | copy-done | bytes 2072
  5.9 37.3 %newton.1 = f32[4,16,128]{2,1,0:T(8,128)S(1)} custom-call(s32[4]{0:T(128)S(1)} %copy-done.8, s32[4,16]{1,0:T(4,128)S(1)} %copy-done.4, s32[4,16]{1,0:T(4,128)S(1)} %copy-done.5, s32[4,16]{1,0:T(4,128)S(1)} %copy-done.6, f32[4,128]{1,0:T(4,128)S(1)} %copy-done.7, f32[4,16,128]{2,1,0:T(8,128)S(1)} %copy-done.1, f32[16,384]{1,0:T(8,128)S(1)} %copy-done.2, ...), custom_call_target="tpu_custom_call" | custom-call | tf_op jit(solution)/shard_map/newton/pallas_call | solution.py:339
  43.2 0.6 %copy.13 = f32[4,16,128]{2,1,0:T(8,128)} copy(f32[4,16,128]{2,1,0:T(8,128)S(1)} %newton.1) | data formatting | bytes 65536
Async XLA Ops:
  0.0 0.7 %copy-start.4 = (s32[4,16]{1,0:T(4,128)S(1)}, s32[4,16]{1,0:T(4,128)}, u32[]{:S(2)}) copy-start(s32[4,16]{1,0:T(4,128)} %demand_ref.1) | copy-start | bytes 772
  0.0 0.7 %copy-start.8 = (s32[4]{0:T(128)S(1)}, s32[4]{0:T(128)}, u32[]{:S(2)}) copy-start(s32[4]{0:T(128)} %sid_ref.1) | copy-start | bytes 52
  0.0 0.7 %copy-start.9 = (f32[128]{0:T(128)S(1)}, f32[128]{0:T(128)}, u32[]{:S(2)}) copy-start(f32[128]{0:T(128)} %param.20) | copy-start | bytes 1540
  0.0 0.7 %copy-start.10 = (f32[128]{0:T(128)S(1)}, f32[128]{0:T(128)}, u32[]{:S(2)}) copy-start(f32[128]{0:T(128)} %param.21) | copy-start | bytes 1540
  0.7 0.9 %copy-start = (f32[128,384]{1,0:T(8,128)S(1)}, f32[128,384]{1,0:T(8,128)}, u32[]{:S(2)}) copy-start(f32[128,384]{1,0:T(8,128)} %rw_ref.1) | copy-start | bytes 589828
  1.6 0.8 %copy-start.1 = (f32[4,16,128]{2,1,0:T(8,128)S(1)}, f32[4,16,128]{2,1,0:T(8,128)}, u32[]{:S(2)}) copy-start(f32[4,16,128]{2,1,0:T(8,128)} %guess_ref.1) | copy-start | bytes 98308
  2.4 0.7 %copy-start.2 = (f32[16,384]{1,0:T(8,128)S(1)}, f32[16,384]{1,0:T(8,128)}, u32[]{:S(2)}) copy-start(f32[16,384]{1,0:T(8,128)} %iw_ref.1) | copy-start | bytes 73732
  3.1 0.7 %copy-start.3 = (f32[16,384]{1,0:T(8,128)S(1)}, f32[16,384]{1,0:T(8,128)}, u32[]{:S(2)}) copy-start(f32[16,384]{1,0:T(8,128)} %table_ref.1) | copy-start | bytes 73732
  3.9 0.7 %copy-start.5 = (s32[4,16]{1,0:T(4,128)S(1)}, s32[4,16]{1,0:T(4,128)}, u32[]{:S(2)}) copy-start(s32[4,16]{1,0:T(4,128)} %lead_ref.1) | copy-start | bytes 772
  4.5 0.7 %copy-start.6 = (s32[4,16]{1,0:T(4,128)S(1)}, s32[4,16]{1,0:T(4,128)}, u32[]{:S(2)}) copy-start(s32[4,16]{1,0:T(4,128)} %review_ref.1) | copy-start | bytes 772
  5.2 0.7 %copy-start.7 = (f32[4,128]{1,0:T(4,128)S(1)}, f32[4,128]{1,0:T(4,128)}, u32[]{:S(2)}) copy-start(f32[4,128]{1,0:T(4,128)} %init_ref.1) | copy-start | bytes 6148
where the time goes:
time: 44.2 us; the launch traced here: 43.8 us
  Pallas kernels  37.3 us (84%)
  local copies, waits for them, and re-layouts  6.51 us (15%)
    pallas_call x1, Pallas kernels, on_device(): pl.pallas_call(kernel, out_shape=jax.ShapeDtypeStruct(guess.shape, F32),...  37.3 us
    unnamed x23, local copies, waits for them, and re-layouts  6.51 us

commit v1 on v0

--- a/solution.py
+++ b/solution.py
@@ -9,7 +9,7 @@
 
 LEAD = 8
 NEWTON = 2
-EXACT = (True, True)
+EXACT = (False, False)
 MESH = pl.DeviceIdType.MESH
 F32 = jnp.float32
 BF16 = jnp.bfloat16
@@ -26,7 +26,7 @@
 
 def dot3(value, w_high, w_low):
     high, low = split(value)
-    return dot(high, w_high) + dot(low, w_high) + dot(high, w_low)
+    return dot(jnp.concatenate([high, low], axis=1), jnp.concatenate([w_high, w_high], axis=0)) + dot(high, w_low)
 
 
 def through(column, matrix):
@@ -39,12 +39,33 @@
 
 
 def kernel(
-    sid_ref, demand_ref, lead_ref, review_ref, init_ref, guess_ref, iw_ref, table_ref, rw_ref, ub_ref, depth_ref,
+    sid_hbm, demand_hbm, lead_hbm, review_hbm, init_hbm, guess_hbm, iw_hbm, table_hbm, rw_hbm, ub_hbm, depth_hbm,
     out_ref,
-    sbuf, held, old, wh, wl, xin, mult, co_z, co_cz, co_n, co_r, err, pre, aff, dsend, dtake, traj,
+    sid_ref, demand_ref, lead_ref, review_ref, init_ref, iw_ref, table_ref, rw_ref, ub_ref, depth_ref, in_sem,
+    sbuf, held, old, wh, wl, xin, mult, co_z, co_cz, co_n, co_r, err, pre, aff, dsend, dtake, traj, reach, reach_row,
     send_sem, rim_sem, recv_sem, rim_recv, chain_send, chain_recv, out_send, out_recv,
 ):
-    scen, periods, hidden = guess_ref.shape
+    scen, periods, hidden = guess_hbm.shape
+    loads = [
+        pltpu.make_async_copy(source, target, in_sem.at[i])
+        for i, (source, target) in enumerate(
+            [
+                (demand_hbm, demand_ref),
+                (lead_hbm, lead_ref),
+                (review_hbm, review_ref),
+                (guess_hbm, sbuf.at[:, :, pl.ds(0, hidden)]),
+                (rw_hbm, rw_ref),
+                (init_hbm, init_ref),
+                (iw_hbm, iw_ref),
+                (table_hbm, table_ref),
+                (ub_hbm, ub_ref),
+                (depth_hbm, depth_ref),
+                (sid_hbm, sid_ref),
+            ]
+        )
+    ]
+    for load in loads:
+        load.start()
     inner = lax.axis_size("tm")
     links = lax.axis_size("slab") * inner // scen
     place = lax.axis_index("slab") * inner + lax.axis_index("tm")
@@ -83,11 +104,12 @@
         picked = jnp.where(diagonal, jnp.broadcast_to(row, square), 0.0)
         return jnp.broadcast_to(jnp.sum(picked, axis=1, keepdims=True), (periods, hidden))
 
+    for load in loads[:4]:
+        load.wait()
     for s in range(scen):
         demand = upright(demand_ref[s : s + 1, :].astype(F32))
         lead = upright(lead_ref[s : s + 1, :].astype(F32))
         review = upright(review_ref[s : s + 1, :].astype(F32))
-        sbuf[s, :, :hidden] = guess_ref[s]
         sbuf[s, :, hidden:] = jnp.where(lane < LEAD, demand, jnp.where(lane < 2 * LEAD, lead, review))
 
     pl.semaphore_wait(
@@ -135,6 +157,8 @@
         for member in range(scen):
             rim(member).start()
 
+    for load in loads[4:]:
+        load.wait()
     held[pl.ds(pl.multiple_of(8 + mine * periods, 8), periods), :] = sbuf[mine]
 
     @pl.when(first)
@@ -174,7 +198,8 @@
         1.0,
         0.0,
     )
-    pad = 16
+    for t in range(periods):
+        aff[t] = jnp.zeros(aff.shape[1:], F32)
 
     for turn in range(NEWTON):
         prior = old[7 : 7 + rows, :]
@@ -201,14 +226,17 @@
                 + co_r[at, :] * rw_ref[:, hidden : 2 * hidden]
             )
             aff[0, b : b + 1, :] = err[at, :]
-        aff[0, scen:, :] = jnp.zeros((pad - scen, hidden), F32)
+            if not EXACT[turn]:
+                aff[0, scen + b : scen + b + 1, :] = err[at, :] - err[at, :].astype(BF16).astype(F32)
+
+        w_both = jnp.concatenate([wh[...], wl[...]], axis=0)
 
         def compose(t, carry):
             x = jnp.concatenate([pre[t - 1], aff[t - 1]], axis=0)
+            high = x.astype(BF16)
+            moved = dot(jnp.concatenate([high, high], axis=1), w_both)
             if EXACT[turn]:
-                moved = dot3(x, wh[...], wl[...])
-            else:
-                moved = dot(x.astype(BF16), wh[...])
+                moved += dot((x - high.astype(F32)).astype(BF16), wh[...])
             for b in range(scen):
                 at = pl.ds(b * periods + t, 1)
                 own = slice(b * hidden, (b + 1) * hidden)
@@ -219,17 +247,33 @@
                     + co_r[at, :] * moved[own, hidden : 2 * hidden]
                 )
                 row = slice(scen * hidden + b, scen * hidden + b + 1)
-                aff[t, b : b + 1, :] = (
+                rest = slice(scen * hidden + scen + b, scen * hidden + scen + b + 1)
+                pushed = moved[row] if EXACT[turn] else moved[row] + moved[rest]
+                value = (
                     co_z[at, :] * x[row]
-                    + co_cz[at, :] * moved[row, :hidden]
-                    + co_n[at, :] * moved[row, 2 * hidden :]
-                    + co_r[at, :] * moved[row, hidden : 2 * hidden]
+                    + co_cz[at, :] * pushed[:, :hidden]
+                    + co_n[at, :] * pushed[:, 2 * hidden :]
+                    + co_r[at, :] * pushed[:, hidden : 2 * hidden]
                     + err[at, :]
                 )
-            aff[t, scen:, :] = jnp.zeros((pad - scen, hidden), F32)
+                aff[t, b : b + 1, :] = value
+                if not EXACT[turn]:
+                    aff[t, scen + b : scen + b + 1, :] = value - value.astype(BF16).astype(F32)
             return carry
 
         lax.fori_loop(1, periods, compose, 0)
+
+        last = periods - 1
+        for b in range(scen):
+            own = slice(b * hidden, (b + 1) * hidden)
+            row = jnp.broadcast_to(aff[last, b : b + 1, :], (8, hidden))
+            if b == 0:
+                reach[0], reach_row[0] = pre[last, own, :], row
+            else:
+                joined = dot3(
+                    jnp.concatenate([reach[b - 1], reach_row[b - 1]], axis=0), *split(pre[last, own, :])
+                )
+                reach[b], reach_row[b] = joined[:hidden], joined[hidden:] + row
 
         onward = pltpu.make_async_remote_copy(
             src_ref=dsend.at[turn],
@@ -249,19 +293,17 @@
             onward.wait_recv()
 
         enter = dtake[turn, 0:1, :]
-        entering = enter
-        columns = []
-        for b in range(scen):
-            column = column_of(entering)
-            columns.append(column)
-            entering = aff[periods - 1, b : b + 1, :] + through(
-                column, pre[periods - 1, b * hidden : (b + 1) * hidden, :]
-            )
-        dsend[turn] = jnp.broadcast_to(entering, (8, hidden))
+        column = column_of(enter)
+        whole = reach_row[scen - 1, 0:1, :] + through(column, reach[scen - 1])
+        dsend[turn] = jnp.broadcast_to(whole, (8, hidden))
 
         @pl.when(jnp.logical_not(final))
         def _():
             onward.start()
+
+        columns = [column]
+        for b in range(scen - 1):
+            columns.append(column_of(reach_row[b, 0:1, :] + through(column, reach[b])))
 
         target = old if turn + 1 < NEWTON else traj
         shift = 8 if turn + 1 < NEWTON else 0
@@ -334,14 +376,23 @@
     scen, periods, hidden = guess.shape
     rows = scen * periods
     vmem = pl.BlockSpec(memory_space=pltpu.VMEM)
+    hbm = pl.BlockSpec(memory_space=pltpu.HBM)
+    operands = (
+        scenario_id, demand, lead_offset, review, initial_state, guess, input_weight, scenario_table,
+        recur_weight, update_bias[None], review_depth[None],
+    )
+    staged = [
+        (pltpu.SMEM if i == 0 else pltpu.VMEM)(o.shape, o.dtype) for i, o in enumerate(operands) if i != 5
+    ]
     dma = pltpu.SemaphoreType.DMA
     tile = pltpu.VMEM((rows, hidden), F32)
     return pl.pallas_call(
         kernel,
         out_shape=jax.ShapeDtypeStruct(guess.shape, F32),
-        in_specs=[pl.BlockSpec(memory_space=pltpu.SMEM)] + [vmem] * 10,
+        in_specs=[hbm] * 11,
         out_specs=vmem,
-        scratch_shapes=[
+        scratch_shapes=staged + [
+            dma((11,)),
             pltpu.VMEM((scen, periods, 2 * hidden), F32),
             pltpu.VMEM((8 + rows, 2 * hidden), F32),
             pltpu.VMEM((8 + rows, hidden), F32),
@@ -354,16 +405,15 @@
             pltpu.VMEM((NEWTON, 8, hidden), F32),
             pltpu.VMEM((NEWTON, 8, hidden), F32),
             tile,
+            pltpu.VMEM((scen, hidden, hidden), F32),
+            pltpu.VMEM((scen, 8, hidden), F32),
             dma((scen,)), dma((scen,)), dma((scen,)), dma(()), dma((NEWTON,)), dma((NEWTON,)), dma((scen,)), dma((scen,)),
         ],
         compiler_params=pltpu.CompilerParams(
-            collective_id=0, has_side_effects=True, vmem_limit_bytes=40 * 1024 * 1024
+            collective_id=0, has_side_effects=True, vmem_limit_bytes=60 * 1024 * 1024
         ),
         name="newton",
-    )(
-        scenario_id, demand, lead_offset, review, initial_state, guess, input_weight, scenario_table,
-        recur_weight, update_bias[None], review_depth[None],
-    )
+    )(*operands)
 
 
 def solution(mesh):

time: 44.2 us -> 30.2 us (0.68)
  Pallas kernels: 37.3 us -> 28.7 us
  local copies, waits for them, and re-layouts: 6.51 us -> 1.38 us
    pallas_call x1, Pallas kernels: 37.3 us -> 28.7 us  [on_device(): pl.pallas_call(kernel, out_shape=jax.ShapeDtypeStruct(guess.shape, F32),...]
    unnamed x23 -> x1, local copies, waits for them, and re-layouts: 6.51 us -> 1.38 us
where the time goes in v1:
time: 30.2 us; the launch traced here: 30.1 us
  Pallas kernels  28.7 us (95%)
  local copies, waits for them, and re-layouts  1.38 us (5%)
    pallas_call x1, Pallas kernels, on_device(): pl.pallas_call(kernel, out_shape=jax.ShapeDtypeStruct(guess.shape, F32),...  28.7 us
    unnamed x1, local copies, waits for them, and re-layouts  1.38 us

profile of v1, /device:TPU:17, one launch (start us, length us, event | category | flops | bytes accessed | tf_op | source)
XLA Modules:
  0.0 30.1 jit_solution(6145392633932637134)
XLA Ops:
  0.0 28.7 %newton.1 = f32[4,16,128]{2,1,0:T(8,128)} custom-call(s32[4]{0:T(128)} %sid_hbm.1, s32[4,16]{1,0:T(4,128)} %demand_hbm.1, s32[4,16]{1,0:T(4,128)} %lead_hbm.1, s32[4,16]{1,0:T(4,128)} %review_hbm.1, f32[4,128]{1,0:T(4,128)} %init_hbm.1, f32[4,16,128]{2,1,0:T(8,128)} %guess_hbm.1, f32[16,384]{1,0:T(8,128)} %iw_hbm.1, f32[16,384]{1,0:T(8,128)} %table_hbm.1, ...), custom_call_target="tpu_custom_call" | custom-call | tf_op jit(solution)/shard_map/newton/pallas_call | solution.py:389
  28.7 1.4 %copy.13 = f32[4,16,128]{2,1,0:T(8,128)} copy(f32[4,16,128]{2,1,0:T(8,128)} %newton.1) | data formatting | bytes 65536

commit v2 on v1

--- a/solution.py
+++ b/solution.py
@@ -261,7 +261,7 @@
                     aff[t, scen + b : scen + b + 1, :] = value - value.astype(BF16).astype(F32)
             return carry
 
-        lax.fori_loop(1, periods, compose, 0)
+        lax.fori_loop(1, periods, compose, 0, unroll=True)
 
         last = periods - 1
         for b in range(scen):

time: 30.2 us -> 25.3 us (0.84)
  Pallas kernels: 28.7 us -> 23.7 us
    pallas_call x1, Pallas kernels: 28.7 us -> 23.7 us  [on_device(): pl.pallas_call(kernel, out_shape=jax.ShapeDtypeStruct(guess.shape, F32),...]
where the time goes in v2:
time: 25.3 us; the launch traced here: 25.1 us
  Pallas kernels  23.7 us (94%)
  local copies, waits for them, and re-layouts  1.38 us (5%)
    pallas_call x1, Pallas kernels, on_device(): pl.pallas_call(kernel, out_shape=jax.ShapeDtypeStruct(guess.shape, F32),...  23.7 us
    unnamed x1, local copies, waits for them, and re-layouts  1.38 us

profile of v2, /device:TPU:17, one launch (start us, length us, event | category | flops | bytes accessed | tf_op | source)
XLA Modules:
  0.0 25.1 jit_solution(15888228903010810156)
XLA Ops:
  0.0 23.7 %newton.1 = f32[4,16,128]{2,1,0:T(8,128)} custom-call(s32[4]{0:T(128)} %sid_hbm.1, s32[4,16]{1,0:T(4,128)} %demand_hbm.1, s32[4,16]{1,0:T(4,128)} %lead_hbm.1, s32[4,16]{1,0:T(4,128)} %review_hbm.1, f32[4,128]{1,0:T(4,128)} %init_hbm.1, f32[4,16,128]{2,1,0:T(8,128)} %guess_hbm.1, f32[16,384]{1,0:T(8,128)} %iw_hbm.1, f32[16,384]{1,0:T(8,128)} %table_hbm.1, ...), custom_call_target="tpu_custom_call" | custom-call | tf_op jit(solution)/shard_map/newton/pallas_call | solution.py:389
  23.7 1.4 %copy.13 = f32[4,16,128]{2,1,0:T(8,128)} copy(f32[4,16,128]{2,1,0:T(8,128)} %newton.1) | data formatting | bytes 65536

commit v3 on v2

--- a/solution.py
+++ b/solution.py
@@ -64,8 +64,6 @@
             ]
         )
     ]
-    for load in loads:
-        load.start()
     inner = lax.axis_size("tm")
     links = lax.axis_size("slab") * inner // scen
     place = lax.axis_index("slab") * inner + lax.axis_index("tm")
@@ -95,6 +93,9 @@
     @pl.when(jnp.logical_not(first) & jnp.logical_not(tail))
     def _():
         pl.semaphore_signal(barrier, inc=1, device_id=device(link - 1, scen - 1), device_id_type=MESH)
+
+    for load in loads:
+        load.start()
 
     square = (periods, periods)
     diagonal = lax.broadcasted_iota(jnp.int32, square, 0) == lax.broadcasted_iota(jnp.int32, square, 1)
@@ -200,6 +201,16 @@
     )
     for t in range(periods):
         aff[t] = jnp.zeros(aff.shape[1:], F32)
+
+    def back(to):
+        return pltpu.make_async_remote_copy(
+            src_ref=traj.at[pl.ds(pl.multiple_of(to * periods, 8), periods)],
+            dst_ref=out_ref.at[mine],
+            send_sem=out_send.at[to],
+            recv_sem=out_recv.at[mine],
+            device_id=device(link, to),
+            device_id_type=MESH,
+        )
 
     for turn in range(NEWTON):
         prior = old[7 : 7 + rows, :]
@@ -317,31 +328,24 @@
                     + aff[t, b : b + 1, :]
                     + through(columns[b], pre[t, b * hidden : (b + 1) * hidden, :])
                 )
-
-    def back(step):
-        to = peer(step)
-        return pltpu.make_async_remote_copy(
-            src_ref=traj.at[pl.ds(pl.multiple_of(to * periods, 8), periods)],
-            dst_ref=out_ref.at[mine],
-            send_sem=out_send.at[step],
-            recv_sem=out_recv.at[scen - step],
-            device_id=device(link, to),
-            device_id_type=MESH,
-        )
+            if turn + 1 == NEWTON:
+
+                @pl.when(mine != b)
+                def _():
+                    back(b).start()
+
 
     def returned(step):
         source = peer(step)
         return pltpu.make_async_remote_copy(
             src_ref=traj.at[pl.ds(0, periods)],
             dst_ref=out_ref.at[source],
-            send_sem=out_send.at[step],
-            recv_sem=out_recv.at[step],
+            send_sem=out_send.at[source],
+            recv_sem=out_recv.at[source],
             device_id=device(link, source),
             device_id_type=MESH,
         )
 
-    for step in range(1, scen):
-        back(step).start()
     out_ref[mine] = traj[pl.ds(pl.multiple_of(mine * periods, 8), periods), :]
 
     for step in range(1, scen):
@@ -365,7 +369,7 @@
             ).wait_send()
 
     for step in range(1, scen):
-        back(step).wait_send()
+        back(peer(step)).wait_send()
         returned(step).wait_recv()
 
 

time: 25.3 us -> 25 us (0.988)
  Pallas kernels: 23.7 us -> 23.3 us
    pallas_call x1, Pallas kernels: 23.7 us -> 23.3 us  [on_device(): pl.pallas_call(kernel, out_shape=jax.ShapeDtypeStruct(guess.shape, F32),...]
where the time goes in v3:
time: 25 us; the launch traced here: 24.7 us
  Pallas kernels  23.3 us (93%)
  local copies, waits for them, and re-layouts  1.38 us (6%)
    pallas_call x1, Pallas kernels, on_device(): pl.pallas_call(kernel, out_shape=jax.ShapeDtypeStruct(guess.shape, F32),...  23.3 us
    unnamed x1, local copies, waits for them, and re-layouts  1.38 us

profile of v3, /device:TPU:17, one launch (start us, length us, event | category | flops | bytes accessed | tf_op | source)
XLA Modules:
  0.0 24.7 jit_solution(2777863973988523131)
XLA Ops:
  0.0 23.3 %newton.1 = f32[4,16,128]{2,1,0:T(8,128)} custom-call(s32[4]{0:T(128)} %sid_hbm.1, s32[4,16]{1,0:T(4,128)} %demand_hbm.1, s32[4,16]{1,0:T(4,128)} %lead_hbm.1, s32[4,16]{1,0:T(4,128)} %review_hbm.1, f32[4,128]{1,0:T(4,128)} %init_hbm.1, f32[4,16,128]{2,1,0:T(8,128)} %guess_hbm.1, f32[16,384]{1,0:T(8,128)} %iw_hbm.1, f32[16,384]{1,0:T(8,128)} %table_hbm.1, ...), custom_call_target="tpu_custom_call" | custom-call | tf_op jit(solution)/shard_map/newton/pallas_call | solution.py:393
  23.3 1.4 %copy.13 = f32[4,16,128]{2,1,0:T(8,128)} copy(f32[4,16,128]{2,1,0:T(8,128)} %newton.1) | data formatting | bytes 65536

commit v4 on v3

--- a/solution.py
+++ b/solution.py
@@ -150,13 +150,13 @@
             device_id_type=MESH,
         )
 
+    @pl.when(tail & jnp.logical_not(final))
+    def _():
+        for member in range(scen):
+            rim(member).start()
+
     for step in range(1, scen):
         exchange(step).start()
-
-    @pl.when(tail & jnp.logical_not(final))
-    def _():
-        for member in range(scen):
-            rim(member).start()
 
     for load in loads[4:]:
         load.wait()
@@ -287,8 +287,8 @@
                 reach[b], reach_row[b] = joined[:hidden], joined[hidden:] + row
 
         onward = pltpu.make_async_remote_copy(
-            src_ref=dsend.at[turn],
-            dst_ref=dtake.at[turn],
+            src_ref=dsend.at[turn, pl.ds(0, 1)],
+            dst_ref=dtake.at[turn, pl.ds(0, 1)],
             send_sem=chain_send.at[turn],
             recv_sem=chain_recv.at[turn],
             device_id=device(link + 1, mine),
@@ -360,8 +360,8 @@
     def _():
         for turn in range(NEWTON):
             pltpu.make_async_remote_copy(
-                src_ref=dsend.at[turn],
-                dst_ref=dtake.at[turn],
+                src_ref=dsend.at[turn, pl.ds(0, 1)],
+                dst_ref=dtake.at[turn, pl.ds(0, 1)],
                 send_sem=chain_send.at[turn],
                 recv_sem=chain_recv.at[turn],
                 device_id=device(link + 1, mine),

time: 25 us -> 24.8 us (level)
  no operation moved by 1% of the time
where the time goes in v4:
time: 24.8 us; the launch traced here: 24.5 us
  Pallas kernels  23.1 us (93%)
  local copies, waits for them, and re-layouts  1.38 us (6%)
    pallas_call x1, Pallas kernels, on_device(): pl.pallas_call(kernel, out_shape=jax.ShapeDtypeStruct(guess.shape, F32),...  23.1 us
    unnamed x1, local copies, waits for them, and re-layouts  1.38 us

profile of v4, /device:TPU:17, one launch (start us, length us, event | category | flops | bytes accessed | tf_op | source)
XLA Modules:
  0.0 24.5 jit_solution(16594178321071404123)
XLA Ops:
  0.0 23.1 %newton.1 = f32[4,16,128]{2,1,0:T(8,128)} custom-call(s32[4]{0:T(128)} %sid_hbm.1, s32[4,16]{1,0:T(4,128)} %demand_hbm.1, s32[4,16]{1,0:T(4,128)} %lead_hbm.1, s32[4,16]{1,0:T(4,128)} %review_hbm.1, f32[4,128]{1,0:T(4,128)} %init_hbm.1, f32[4,16,128]{2,1,0:T(8,128)} %guess_hbm.1, f32[16,384]{1,0:T(8,128)} %iw_hbm.1, f32[16,384]{1,0:T(8,128)} %table_hbm.1, ...), custom_call_target="tpu_custom_call" | custom-call | tf_op jit(solution)/shard_map/newton/pallas_call | solution.py:393
  23.1 1.4 %copy.13 = f32[4,16,128]{2,1,0:T(8,128)} copy(f32[4,16,128]{2,1,0:T(8,128)} %newton.1) | data formatting | bytes 65536
